TPU v7x, 512 devices: a whole 4x4x16 slice. The times are simulated.
512 devices in a mesh: tok: 16 (over z), col: 32 (over x, y, core).
Axes of the slice: x: 4, y: 4, z: 16, core: 2. Of those that a mesh axis runs over, the one named last changes fastest.
Arguments:
- acts: bfloat16 [8192, 28672], P('tok', 'col'), may hold values from -6 to 6
- residual: float32 [8192, 8192], P('tok', 'col'), may hold values from -6 to 6
- weights: bfloat16 [32, 896, 8192], P(None, 'tok', 'col'), may hold values from -6 to 6
- order: int32 [4], replicated, may hold values from 0 to 31
- rate: float32 [32], replicated, may hold values from 0.1 to 0.4
- penalty: float32 [32], replicated, may hold values from 0.4 to 1.2
Outputs:
- pruned: float32 [32, 896, 8192], P(None, 'tok', 'col')
- resid_out: float32 [8192, 8192], P('tok', 'col')
Inputs may be any that keep to these rules, and one draw needn't show every extreme that they name: `order`: block indices, repeats allowed.
All inputs are finite; a program needn't handle non-finite values.
Results may differ from a plain program's by a relative error of at most 0.0054.
Values may be sent and summed in bfloat16 or wider, within the bound.
A program may use at most 64 MiB of HBM per device.

v0:
```python
import math

import jax
import jax.numpy as jnp
from jax import lax
from jax.sharding import PartitionSpec as P

D = 8192
CH = 28672
STEPS = 4


def from_root(block, axis, holder):
    block = jnp.where(lax.axis_index(axis) == holder, block, jnp.zeros_like(block))
    return lax.psum(block, axis)


def body(acts, residual, weights, order, rate, penalty):
    tok_rows = acts.shape[0]
    scale = math.sqrt(CH)
    thresh_unit = math.sqrt(D)
    eta_unit = float(CH) / float(tok_rows * lax.axis_size("tok"))
    state = weights.astype(jnp.float32)
    resid = residual
    for step in range(STEPS):
        which = order[step]
        block_acts = from_root(acts, "col", which)
        lowered = resid.astype(jnp.bfloat16)
        partial_grad = lax.dot_general(
            block_acts, lowered, (((0,), (0,)), ((), ())), preferred_element_type=jnp.float32
        )
        current = lax.dynamic_index_in_dim(state, which, 0, keepdims=False)
        step_size = rate[which] * eta_unit
        limit = penalty[which] * thresh_unit
        grad = lax.psum_scatter(partial_grad, "tok", scatter_dimension=0, tiled=True) / scale
        shifted = current - step_size * grad
        sums = lax.psum(jnp.sum(shifted * shifted, axis=1), "col")
        factor = jnp.maximum(0.0, 1.0 - limit / jnp.sqrt(sums + 1e-06))
        fresh = factor[:, None] * shifted
        local_change = (fresh - current).astype(jnp.bfloat16)
        state = lax.dynamic_update_index_in_dim(state, fresh, which, 0)
        change = lax.all_gather(local_change, "tok", axis=0, tiled=True)
        resid = resid + jnp.dot(block_acts, change, preferred_element_type=jnp.float32) / scale
    return (state, resid)


def solution(mesh):
    in_specs = (P("tok", "col"), P("tok", "col"), P(None, "tok", "col"), P(), P(), P())
    out_specs = (P(None, "tok", "col"), P("tok", "col"))
    return jax.shard_map(body, mesh=mesh, in_specs=in_specs, out_specs=out_specs, check_vma=False)
```

profile of v0, /device:TPU:1, one launch (start us, length us, event | category | flops | bytes accessed | tf_op | source)
XLA Modules:
  0.0 812.7 jit_solution(8121737015502011051)
XLA Ops:
  7.2 1.4 fusion.18
  11.1 3.1 broadcast_select_fusion
  14.3 146.9 %all-reduce.3.cloned.1.call-done = (bf16[512,896]{1,0:T(8,128)(2,1)}, bf16[512,896]{1,0:T(8,128)(2,1)}, bf16[512,896]{1,0:T(8,128)(2,1)}, bf16[512,896]{1,0:T(8,128)(2,1)}) async-done(((bf16[512,896]{1,0:T(8,128)(2,1)}, bf16[512,896]{1,0:T(8,128)(2,1)}, bf16[512,896]{1,0:T(8,128)(2,1)}, bf16[512,896]{1,0:T(8,128)(2,1)}), (bf16[512,896]{1,0:T(8,128)(2,1)}, bf16[512,896]{1,0:T(8,128)(2,1)}, ...) | async-done | bytes 3670032 | tf_op jit(solution)/shard_map/psum | solution.py:15
  161.2 2.5 fusion.10
  168.8 1.4 convert_element_type.27
  175.4 48.4 %reduce-scatter.5.cloned.1.call-done = f32[56,256]{1,0:T(8,128)} async-done(((f32[896,256]{1,0:T(8,128)}), f32[56,256]{1,0:T(8,128)}) %reduce-scatter.5.cloned.1.call-update) | async-done | bytes 57360 | tf_op jit(solution)/shard_map/reduce_scatter | solution.py:35
  223.8 1.0 multiply_reduce_fusion.3
  224.8 72.9 %psum.57 = f32[56]{0:T(128)S(1)} all-reduce(f32[56]{0:T(128)S(1)} %get-tuple-element.12), channel_id=1, replica_groups=mesh['tok'=16,'col'=32] {'col'}, use_global_device_ids=true, to_apply=%region_3.4 | all-reduce | flops 56 | bytes 448 | tf_op jit(solution)/shard_map/psum | solution.py:37
  298.6 23.3 %all_gather.12 = bf16[896,256]{1,0:T(8,128)(2,1)S(1)} all-gather(bf16[56,256]{1,0:T(8,128)(2,1)S(1)} %fusion.15), channel_id=1, replica_groups=mesh['tok'=16,'col'=32] {'tok'}, dimensions={0}, use_global_device_ids=true | all-gather | bytes 487424 | tf_op jit(solution)/shard_map/all_gather | solution.py:42
  322.3 1.4 fusion.8
  325.6 58.5 %reduce-scatter.7.cloned.1.call-done = f32[56,256]{1,0:T(8,128)} async-done(((f32[896,256]{1,0:T(8,128)}), f32[56,256]{1,0:T(8,128)}) %reduce-scatter.7.cloned.1.call-update) | async-done | bytes 57360 | tf_op jit(solution)/shard_map/reduce_scatter | solution.py:35
  384.1 1.0 multiply_reduce_fusion.2
  385.1 73.3 %psum.59 = f32[56]{0:T(128)S(1)} all-reduce(f32[56]{0:T(128)S(1)} %get-tuple-element.10), channel_id=1, replica_groups=mesh['tok'=16,'col'=32] {'col'}, use_global_device_ids=true, to_apply=%region_7.8 | all-reduce | flops 56 | bytes 448 | tf_op jit(solution)/shard_map/psum | solution.py:37
  459.3 23.2 %all_gather.13 = bf16[896,256]{1,0:T(8,128)(2,1)S(1)} all-gather(bf16[56,256]{1,0:T(8,128)(2,1)S(1)} %fusion.14), channel_id=1, replica_groups=mesh['tok'=16,'col'=32] {'tok'}, dimensions={0}, use_global_device_ids=true | all-gather | bytes 487424 | tf_op jit(solution)/shard_map/all_gather | solution.py:42
  482.9 1.4 fusion.6
  486.5 58.7 %reduce-scatter.9.cloned.1.call-done = f32[56,256]{1,0:T(8,128)} async-done(((f32[896,256]{1,0:T(8,128)}), f32[56,256]{1,0:T(8,128)}) %reduce-scatter.9.cloned.1.call-update) | async-done | bytes 57360 | tf_op jit(solution)/shard_map/reduce_scatter | solution.py:35
  545.2 1.0 multiply_reduce_fusion.1
  546.1 72.9 %psum.61 = f32[56]{0:T(128)S(1)} all-reduce(f32[56]{0:T(128)S(1)} %get-tuple-element.8), channel_id=1, replica_groups=mesh['tok'=16,'col'=32] {'col'}, use_global_device_ids=true, to_apply=%region_11.12 | all-reduce | flops 56 | bytes 448 | tf_op jit(solution)/shard_map/psum | solution.py:37
  619.9 23.6 %all_gather.14 = bf16[896,256]{1,0:T(8,128)(2,1)S(1)} all-gather(bf16[56,256]{1,0:T(8,128)(2,1)S(1)} %fusion.13), channel_id=1, replica_groups=mesh['tok'=16,'col'=32] {'tok'}, dimensions={0}, use_global_device_ids=true | all-gather | bytes 487424 | tf_op jit(solution)/shard_map/all_gather | solution.py:42
  644.0 1.4 fusion.4
  647.4 58.7 %reduce-scatter.11.cloned.1.call-done = f32[56,256]{1,0:T(8,128)} async-done(((f32[896,256]{1,0:T(8,128)}), f32[56,256]{1,0:T(8,128)}) %reduce-scatter.11.cloned.1.call-update) | async-done | bytes 57360 | tf_op jit(solution)/shard_map/reduce_scatter | solution.py:35
  707.1 72.5 %psum.63 = f32[56]{0:T(128)S(1)} all-reduce(f32[56]{0:T(128)S(1)} %get-tuple-element.6), channel_id=1, replica_groups=mesh['tok'=16,'col'=32] {'col'}, use_global_device_ids=true, to_apply=%region_15.16 | all-reduce | flops 56 | bytes 448 | tf_op jit(solution)/shard_map/psum | solution.py:37
  781.2 23.7 %all_gather.15 = bf16[896,256]{1,0:T(8,128)(2,1)S(1)} all-gather(bf16[56,256]{1,0:T(8,128)(2,1)S(1)} %fusion.12), channel_id=1, replica_groups=mesh['tok'=16,'col'=32] {'tok'}, dimensions={0}, use_global_device_ids=true | all-gather | bytes 487424 | tf_op jit(solution)/shard_map/all_gather | solution.py:42
  805.0 1.2 fusion.3
  (44 shorter events, 10.4 us)
Async XLA Ops:
  7.2 154.0 %all-reduce.3.cloned.1.call-start = ((), (), s32[]{:S(2)}) async-start(), calls=%async_computation.8 | async-start | bytes 7340032 | tf_op jit(solution)/shard_map/psum | solution.py:15
  14.2 147.0 %copy-start.4 = (f32[512,256]{1,0:T(8,128)S(1)}, f32[512,256]{1,0:T(8,128)}, u32[]{:S(2)}) copy-start(f32[512,256]{1,0:T(8,128)} %param.7) | copy-start | bytes 1572868
  14.2 154.6 %copy-start.5 = (bf16[32,56,256]{2,1,0:T(8,128)(2,1)S(1)}, bf16[32,56,256]{2,1,0:T(8,128)(2,1)}, u32[]{:S(2)}) copy-start(bf16[32,56,256]{2,1,0:T(8,128)(2,1)} %param.8) | copy-start | bytes 2752516
  14.3 209.6 %reduce-scatter.5.cloned.1.call-start = ((), (), s32[]{:S(2)}) async-start(), calls=%async_computation.4 | async-start | bytes 974848 | tf_op jit(solution)/shard_map/reduce_scatter | solution.py:35
  163.7 9.0 %copy-start.6 = (f32[32]{0:T(128)S(1)}, f32[32]{0:T(128)}, u32[]{:S(2)}) copy-start(f32[32]{0:T(128)} %param.10) | copy-start | bytes 388
  163.7 10.3 %copy-start.7 = (f32[32]{0:T(128)S(1)}, f32[32]{0:T(128)}, u32[]{:S(2)}) copy-start(f32[32]{0:T(128)} %param.11) | copy-start | bytes 388
  163.8 158.1 %copy-start.3 = (bf16[512,896]{1,0:T(8,128)(2,1)S(1)}, bf16[512,896]{1,0:T(8,128)(2,1)}, u32[]{:S(2)}) copy-start(bf16[512,896]{1,0:T(8,128)(2,1)} %get-tuple-element.2) | copy-start | bytes 2752516
  163.8 220.4 %reduce-scatter.7.cloned.1.call-start = ((), (), s32[]{:S(2)}) async-start(), calls=%async_computation.5 | async-start | bytes 974848 | tf_op jit(solution)/shard_map/reduce_scatter | solution.py:35
  170.2 152.1 %copy-start.2 = (bf16[512,896]{1,0:T(8,128)(2,1)S(1)}, bf16[512,896]{1,0:T(8,128)(2,1)}, u32[]{:S(2)}) copy-start(bf16[512,896]{1,0:T(8,128)(2,1)} %get-tuple-element.3) | copy-start | bytes 2752516
  323.7 159.2 %copy-start.1 = (bf16[512,896]{1,0:T(8,128)(2,1)S(1)}, bf16[512,896]{1,0:T(8,128)(2,1)}, u32[]{:S(2)}) copy-start(bf16[512,896]{1,0:T(8,128)(2,1)} %get-tuple-element.4) | copy-start | bytes 2752516
  323.7 221.5 %reduce-scatter.9.cloned.1.call-start = ((), (), s32[]{:S(2)}) async-start(), calls=%async_computation.6 | async-start | bytes 974848 | tf_op jit(solution)/shard_map/reduce_scatter | solution.py:35
  484.4 159.7 %copy-start = (bf16[512,896]{1,0:T(8,128)(2,1)S(1)}, bf16[512,896]{1,0:T(8,128)(2,1)}, u32[]{:S(2)}) copy-start(bf16[512,896]{1,0:T(8,128)(2,1)} %get-tuple-element.5) | copy-start | bytes 2752516
  484.4 221.8 %reduce-scatter.11.cloned.1.call-start = ((), (), s32[]{:S(2)}) async-start(), calls=%async_computation.7 | async-start | bytes 974848 | tf_op jit(solution)/shard_map/reduce_scatter | solution.py:35
Sparse Core Ops, SparseCore 0:
  14.4 146.7 all-reduce.2
  164.0 59.7 reduce-scatter.4
  323.8 60.2 reduce-scatter.6
  484.5 60.6 reduce-scatter.8
  645.6 60.5 reduce-scatter.10
where the time goes:
time: 818 us; the launch traced here: 813 us
  blocking collectives  385 us (47%)
  waiting for transfers between devices  371 us (45%)
  between operations  29 us (4%)
  other arithmetic  14.8 us (2%)
  matrix products  9.26 us (1%)
    psum x4, blocking collectives, body(): sums = lax.psum(jnp.sum(shifted * shifted, axis=1), 'col')  292 us
    reduce_scatter x4, waiting for transfers between devices, body(): lax.psum_scatter(partial_grad, 'tok', scatter_dimension=0, tiled=True)  224 us
    psum x1, waiting for transfers between devices, from_root(): return lax.psum(block, axis)  147 us
    all_gather x4, blocking collectives, body(): change = lax.all_gather(local_change, 'tok', axis=0, tiled=True)  93.8 us
  transfers between devices with their start and end apart: 5, of which 5 were waited for; matrix products, arithmetic and copies ran while one was open for 1% of the time, Pallas kernels for 0%

commit v1 on v0

v1 whole, which is shorter than its diff:
```python
import math

import jax
import jax.numpy as jnp
from jax import lax
from jax.experimental import pallas as pl
from jax.experimental.pallas import tpu as pltpu
from jax.sharding import PartitionSpec as P

D = 8192
CH = 28672
STEPS = 4
NBLK = 32
BLOCK = 896
TOKENS = 8192
NZ = 16
NCOL = 32
ROWS = BLOCK // NZ
COLS = D // NCOL
PIECE = TOKENS // NZ // NCOL
HALF = COLS // 2
CHUNK = (2 * ROWS, HALF)
FAR = (0, 4, -4, 8)
FAR_ORDER = (3, 1, 2)
MESH = pl.DeviceIdType.MESH
F32 = jnp.float32
BF16 = jnp.bfloat16


def fold(rows):
    return jnp.concatenate([rows[:, :HALF], rows[:, HALF:]], axis=0)


def unfold(chunk):
    wide = chunk.astype(F32)
    return jnp.concatenate([wide[:ROWS], wide[ROWS:]], axis=1)


def kernel(
    order_ref, rate_ref, penalty_ref, acts_ref, resid_ref, weights_ref,
    fresh_ref, out_ref,
    pieces, blocks, grad, near_out, near_in, far_out, far_in, sums, gathered, change,
    a2a_s, a2a_r, line_s, line_r, plane_s, plane_r, twin_s, twin_r,
    rn_s, rn_r, rf_s, rf_r, sum_s, sum_r, gf_s, gf_r, gn_s, gn_r,
):
    z = lax.axis_index("tok")
    q = lax.axis_index("col")
    core = lax.rem(q, 2)
    y = lax.rem(q // 2, 4)
    x = q // 8
    near = (0, 1, -1, 2 - 4 * core)
    pending = []

    def at_z(offset):
        return {"tok": lax.rem(z + offset + 2 * NZ, NZ)}

    def at_col(i):
        return {"col": lax.rem(q + i, NCOL)}

    def send(src, dst, ssem, rsem, where):
        copy = pltpu.make_async_remote_copy(
            src_ref=src, dst_ref=dst, send_sem=ssem, recv_sem=rsem, device_id=where, device_id_type=MESH
        )
        copy.start()
        pending.append(copy)
        return copy

    barrier = pltpu.get_barrier_semaphore()

    @pl.loop(1, NCOL)
    def _(i):
        pl.semaphore_signal(barrier, inc=1, device_id=at_col(i), device_id_type=MESH)

    for offset in (1, -1, 2, -2, 4, -4, 8):
        pl.semaphore_signal(barrier, inc=1, device_id=at_z(offset), device_id_type=MESH)
    pl.semaphore_wait(barrier, NCOL - 1 + 7)

    def piece_copy(i):
        peer = lax.rem(q + i, NCOL)
        return pltpu.make_async_remote_copy(
            src_ref=acts_ref.at[pl.ds(pl.multiple_of(peer * PIECE, PIECE), PIECE)],
            dst_ref=pieces.at[q],
            send_sem=a2a_s.at[i],
            recv_sem=a2a_r.at[i],
            device_id=at_col(i),
            device_id_type=MESH,
        )

    @pl.loop(1, NCOL)
    def _(i):
        piece_copy(i).start()

    pieces[q] = acts_ref[pl.ds(pl.multiple_of(q * PIECE, PIECE), PIECE), :]
    out_ref[...] = resid_ref[...]

    @pl.loop(1, NCOL)
    def _(i):
        piece_copy(i).wait()

    def peer_x(i):
        return {"col": (lax.rem(x + i, 4) * 4 + y) * 2 + core}

    def peer_y(i):
        return {"col": (x * 4 + lax.rem(y + i, 4)) * 2 + core}

    for k in range(STEPS):
        blocks[k, x, y, core] = pieces[order_ref[k]]
    line = {}
    for k in range(STEPS):
        mine = blocks.at[k, x, y, core]
        first = peer_x if k % 2 == 0 else peer_y
        line[k] = [send(mine, mine, line_s.at[k, i], line_r.at[k, i], first(i)) for i in (1, 3, 2)]

    plane, twin = {}, {}

    def start_plane(k):
        for copy in line[k]:
            copy.wait_recv()
        mine = blocks.at[k, :, y, core] if k % 2 == 0 else blocks.at[k, x, :, core]
        second = peer_y if k % 2 == 0 else peer_x
        plane[k] = [send(mine, mine, plane_s.at[k, i], plane_r.at[k, i], second(i)) for i in (1, 3, 2)]

    def start_twin(k):
        for copy in plane[k]:
            copy.wait_recv()
        mine = blocks.at[k, :, :, core]
        twin[k] = send(mine, mine, twin_s.at[k], twin_r.at[k], {"col": q + 1 - 2 * core})

    start_plane(0)
    start_plane(1)
    start_twin(0)

    scale = math.sqrt(CH)
    eta_unit = float(CH) / float(TOKENS)
    thresh_unit = math.sqrt(D)
    for k in range(STEPS):
        twin[k].wait_recv()
        block_acts = blocks[k].reshape(TOKENS // NZ, BLOCK)
        lowered = out_ref[...].astype(BF16)
        grad[...] = lax.dot_general(
            block_acts, lowered, (((0,), (0,)), ((), ())), preferred_element_type=F32
        )

        def partial(a, b):
            owner = lax.rem(z + FAR[a] + near[b] + 2 * NZ, NZ)
            return fold(grad[pl.ds(pl.multiple_of(owner * ROWS, 8), ROWS), :])

        near_copies, far_copies = {}, []
        for a in FAR_ORDER + (0,):
            for b in (1, 2, 3):
                near_out[k, a, b] = partial(a, b).astype(BF16)
                near_copies[a, b] = send(
                    near_out.at[k, a, b], near_in.at[k, a, b], rn_s.at[k, a, b], rn_r.at[k, a, b], at_z(near[b])
                )
        if k + 2 < STEPS:
            start_plane(k + 2)
        if k + 1 < STEPS:
            start_twin(k + 1)
        for a in FAR_ORDER + (0,):
            total = partial(a, 0)
            for b in (1, 2, 3):
                near_copies[a, b].wait_recv()
                total = total + near_in[k, a, b].astype(F32)
            if a:
                far_out[k, a] = total.astype(BF16)
                far_copies.append(
                    send(far_out.at[k, a], far_in.at[k, a], rf_s.at[k, a], rf_r.at[k, a], at_z(FAR[a]))
                )
        for a, copy in zip(FAR_ORDER, far_copies):
            copy.wait_recv()
            total = total + far_in[k, a].astype(F32)
        mean_grad = jnp.concatenate([total[:ROWS], total[ROWS:]], axis=1) / scale

        which = order_ref[k]
        current = weights_ref[which].astype(F32)
        for j in range(k):
            current = jnp.where(order_ref[j] == which, fresh_ref[j], current)
        shifted = current - (rate_ref[which] * eta_unit) * mean_grad
        square = shifted * shifted
        square = square[:, :HALF] + square[:, HALF:]
        square = jnp.concatenate([square, jnp.zeros((HALF - ROWS, HALF), F32)], axis=0)
        sums[k, q] = jnp.broadcast_to(jnp.sum(square.T, axis=0, keepdims=True), (8, HALF))

        def sum_copy(i):
            return pltpu.make_async_remote_copy(
                src_ref=sums.at[k, q],
                dst_ref=sums.at[k, q],
                send_sem=sum_s.at[k, i],
                recv_sem=sum_r.at[k, i],
                device_id=at_col(i),
                device_id_type=MESH,
            )

        @pl.loop(1, NCOL)
        def _(i):
            sum_copy(i).start()

        @pl.loop(1, NCOL)
        def _(i):
            sum_copy(i).wait()

        whole = jnp.sum(sums[k], axis=0)
        limit = penalty_ref[which] * thresh_unit
        factor = jnp.maximum(0.0, 1.0 - limit / jnp.sqrt(whole + 1e-06))
        factor = jnp.broadcast_to(factor[:1], (HALF, HALF)).T[:ROWS]
        fresh = jnp.concatenate([factor, factor], axis=1) * shifted
        fresh_ref[k] = fresh

        gathered[k, 0, 0] = fold(fresh - current).astype(BF16)
        mine = gathered.at[k, 0, 0]
        far_moves = {
            a: send(mine, gathered.at[k, a, 0], gf_s.at[k, a], gf_r.at[k, a], at_z(FAR[a])) for a in FAR_ORDER
        }
        near_moves = []
        for a in (0, 1, 2, 3):
            if a:
                far_moves[a].wait_recv()
            for b in (1, 2, 3):
                near_moves.append(
                    send(
                        gathered.at[k, a, 0], gathered.at[k, a, b], gn_s.at[k, a, b], gn_r.at[k, a, b], at_z(near[b])
                    )
                )
        for copy in near_moves:
            copy.wait_recv()
        for a in range(4):
            for b in range(4):
                source = lax.rem(z - FAR[a] - near[b] + 2 * NZ, NZ)
                change[pl.ds(pl.multiple_of(source * ROWS, 8), ROWS), :] = unfold(gathered[k, a, b])
        out_ref[...] = out_ref[...] + (
            jnp.dot(block_acts, change[...].astype(BF16), preferred_element_type=F32) / scale
        )
    for copy in pending:
        copy.wait_send()


def place_kernel(order_ref, weights_ref, fresh_ref, out_ref):
    out_ref[...] = weights_ref[...].astype(F32)
    for k in range(STEPS):
        out_ref[order_ref[k]] = fresh_ref[k]


def body(acts, residual, weights, order, rate, penalty):
    smem = pl.BlockSpec(memory_space=pltpu.SMEM)
    vmem = pl.BlockSpec(memory_space=pltpu.VMEM)
    sems = pltpu.SemaphoreType.DMA
    fresh, resid = pl.pallas_call(
        kernel,
        out_shape=(
            jax.ShapeDtypeStruct((STEPS, ROWS, COLS), F32),
            jax.ShapeDtypeStruct(residual.shape, F32),
        ),
        in_specs=[smem, smem, smem, vmem, vmem, vmem],
        out_specs=(vmem, vmem),
        scratch_shapes=[
            pltpu.VMEM((NCOL, PIECE, BLOCK), BF16),
            pltpu.VMEM((STEPS, 4, 4, 2, PIECE, BLOCK), BF16),
            pltpu.VMEM((BLOCK, COLS), F32),
            pltpu.VMEM((STEPS, 4, 4) + CHUNK, BF16),
            pltpu.VMEM((STEPS, 4, 4) + CHUNK, BF16),
            pltpu.VMEM((STEPS, 4) + CHUNK, BF16),
            pltpu.VMEM((STEPS, 4) + CHUNK, BF16),
            pltpu.VMEM((STEPS, NCOL, 8, HALF), F32),
            pltpu.VMEM((STEPS, 4, 4) + CHUNK, BF16),
            pltpu.VMEM((BLOCK, COLS), F32),
            sems((NCOL,)), sems((NCOL,)),
            sems((STEPS, 4)), sems((STEPS, 4)), sems((STEPS, 4)), sems((STEPS, 4)),
            sems((STEPS,)), sems((STEPS,)),
            sems((STEPS, 4, 4)), sems((STEPS, 4, 4)), sems((STEPS, 4)), sems((STEPS, 4)),
            sems((STEPS, NCOL)), sems((STEPS, NCOL)),
            sems((STEPS, 4)), sems((STEPS, 4)), sems((STEPS, 4, 4)), sems((STEPS, 4, 4)),
        ],
        compiler_params=pltpu.CompilerParams(
            collective_id=0, has_side_effects=True, vmem_limit_bytes=48 * 1024 * 1024
        ),
        name="steps",
    )(order, rate, penalty, acts, residual, weights)
    pruned = pl.pallas_call(
        place_kernel,
        out_shape=jax.ShapeDtypeStruct(weights.shape, F32),
        in_specs=[smem, vmem, vmem],
        out_specs=vmem,
        compiler_params=pltpu.CompilerParams(vmem_limit_bytes=16 * 1024 * 1024),
        name="place",
    )(order, weights, fresh)
    return (pruned, resid)


def solution(mesh):
    in_specs = (P("tok", "col"), P("tok", "col"), P(None, "tok", "col"), P(), P(), P())
    out_specs = (P(None, "tok", "col"), P("tok", "col"))
    return jax.shard_map(body, mesh=mesh, in_specs=in_specs, out_specs=out_specs, check_vma=False)
```

time: 818 us -> 201 us (0.25)
  blocking collectives: 385 us -> 0 us
  waiting for transfers between devices: 371 us -> 0 us
  Pallas kernels: 0 us -> 192 us
  between operations: 29 us -> 0.65 us
  other arithmetic: 14.8 us -> 0 us
  matrix products: 9.26 us -> 0 us
    psum x4 -> x0, blocking collectives: 292 us -> none  [body(): sums = lax.psum(jnp.sum(shifted * shifted, axis=1), 'col')]
    reduce_scatter x4 -> x0, waiting for transfers between devices: 224 us -> none  [body(): lax.psum_scatter(partial_grad, 'tok', scatter_dimension=0, tiled=True)]
    pallas_call x0 -> x2, Pallas kernels: none -> 192 us  [the longest x1 190 us: body(): pl.pallas_call(kernel, out_shape=(jax.ShapeDtypeStruct((STEPS, ROWS, COLS...]
    psum x1 -> x0, waiting for transfers between devices: 147 us -> none  [from_root(): return lax.psum(block, axis)]
    all_gather x4 -> x0, blocking collectives: 93.8 us -> none  [body(): change = lax.all_gather(local_change, 'tok', axis=0, tiled=True)]
    dot_general x8 -> x0, matrix products: 9.26 us -> none  [the longest x4 6.7 us: body(): lax.dot_general(block_acts, lowered, (((0,), (0,)), ((), ())), preferred_...]
  transfers between devices with their start and end apart: 5 -> 0, of which waited for: 5 -> 0; matrix products, arithmetic and copies ran while one was open for 1% -> 0% of each run, Pallas kernels for 0% -> 0%
where the time goes in v1:
time: 201 us; the launch traced here: 199 us
  Pallas kernels  192 us (96%)
  local copies, waits for them, and re-layouts  6.15 us (3%)
    pallas_call x1, Pallas kernels, body(): pl.pallas_call(kernel, out_shape=(jax.ShapeDtypeStruct((STEPS, ROWS, COLS...  190 us
    unnamed x13, local copies, waits for them, and re-layouts  6.15 us

profile of v1, /device:TPU:1, one launch (start us, length us, event | category | flops | bytes accessed | tf_op | source)
XLA Modules:
  0.0 199.1 jit_solution(3815418490482239657)
XLA Ops:
  0.6 0.0 copy-start
  0.6 1.2 copy-done
  1.8 0.0 copy-start.1
  1.8 1.2 copy-done.1
  3.0 0.0 copy-start.2
  3.0 1.0 copy-done.2
  4.0 0.0 copy-start.3
  4.0 0.7 copy-done.3
  4.7 0.0 copy-start.4
  4.7 0.7 copy-done.4
  5.3 0.0 copy-start.5
  5.3 0.7 copy-done.5
  6.0 190.4 %steps.1 = (f32[4,56,256]{2,1,0:T(8,128)S(1)}, f32[512,256]{1,0:T(8,128)S(1)}) custom-call(s32[4]{0:T(128)S(1)} %copy-done.3, f32[32]{0:T(128)S(1)} %copy-done.4, f32[32]{0:T(128)S(1)} %copy-done.5, bf16[512,896]{1,0:T(8,128)(2,1)S(1)} %copy-done.1, f32[512,256]{1,0:T(8,128)S(1)} %copy-done.2, bf16[32,56,256]{2,1,0:T(8,128)(2,1)S(1)} %copy-done), custom_call_target="tpu_custom_call" | custom-call | tf_op jit(solution)/shard_map/steps/pallas_call | solution.py:247
  196.4 1.9 place.1
  198.3 0.8 copy.9
Async XLA Ops:
  0.6 1.2 copy-start
  1.8 1.2 copy-start.1
  3.0 1.0 copy-start.2
  4.0 0.7 copy-start.3
  4.7 0.7 copy-start.4
  5.3 0.7 copy-start.5

commit v2 on v1

v2 whole, which is shorter than its diff:
```python
import math

import jax
import jax.numpy as jnp
from jax import lax
from jax.experimental import pallas as pl
from jax.experimental.pallas import tpu as pltpu
from jax.sharding import PartitionSpec as P

D = 8192
CH = 28672
STEPS = 4
NBLK = 32
BLOCK = 896
TOKENS = 8192
NZ = 16
NCOL = 32
ROWS = BLOCK // NZ
COLS = D // NCOL
PIECE = TOKENS // NZ // NCOL
HALF = COLS // 2
CHUNK = (2 * ROWS, HALF)
FAR = (0, 4, -4, 8)
FAR_ORDER = (3, 1, 2)
MESH = pl.DeviceIdType.MESH
F32 = jnp.float32
BF16 = jnp.bfloat16


def fold(rows):
    return jnp.concatenate([rows[:, :HALF], rows[:, HALF:]], axis=0)


def unfold(chunk):
    wide = chunk.astype(F32)
    return jnp.concatenate([wide[:ROWS], wide[ROWS:]], axis=1)


def kernel(
    order_hbm, rate_hbm, penalty_hbm, acts_ref, resid_ref, weights_hbm,
    fresh_ref, out_ref,
    order_ref, rate_ref, penalty_ref, weights_ref,
    pieces, blocks, grad, near_out, near_in, far_out, far_in, sums, gathered, change,
    load_sems, a2a_r, line_r, plane_r, twin_r, near_r, far_r, sum_r, gf_r, gn_r,
    a2a_s, line_s, plane_s, twin_s, near_s, far_s, sum_s, gf_s, gn_s,
):
    z = lax.axis_index("tok")
    q = lax.axis_index("col")
    core = lax.rem(q, 2)
    y = lax.rem(q // 2, 4)
    x = q // 8
    near = (0, 1, -1, 2 - 4 * core)

    def at_z(offset):
        return {"tok": lax.rem(z + offset + 2 * NZ, NZ)}

    def at_col(i):
        return {"col": lax.rem(q + i, NCOL)}

    def send(src, dst, ssem, rsem, where):
        copy = pltpu.make_async_remote_copy(
            src_ref=src, dst_ref=dst, send_sem=ssem, recv_sem=rsem, device_id=where, device_id_type=MESH
        )
        copy.start()
        return copy

    def recv(ref, sem):
        pltpu.make_async_remote_copy(ref, ref, a2a_s, sem, device_id=at_z(1), device_id_type=MESH).wait_recv()

    def sent(ref, sem):
        pltpu.make_async_remote_copy(ref, ref, sem, a2a_r, device_id=at_z(1), device_id_type=MESH).wait_send()

    own_rows = pl.ds(pl.multiple_of(q * PIECE, PIECE), PIECE)
    loads = [
        pltpu.make_async_copy(src, dst, load_sems.at[i])
        for i, (src, dst) in enumerate((
            (acts_ref.at[own_rows], pieces.at[q]),
            (order_hbm, order_ref),
            (rate_hbm, rate_ref),
            (penalty_hbm, penalty_ref),
            (resid_ref, out_ref),
            (weights_hbm, weights_ref),
        ))
    ]
    for copy in loads:
        copy.start()

    barrier = pltpu.get_barrier_semaphore()

    @pl.loop(1, NCOL)
    def _(i):
        pl.semaphore_signal(barrier, inc=1, device_id=at_col(i), device_id_type=MESH)

    for offset in (1, -1, 2, -2, 4, -4, 8):
        pl.semaphore_signal(barrier, inc=1, device_id=at_z(offset), device_id_type=MESH)
    pl.semaphore_wait(barrier, NCOL - 1 + 7)

    def piece_copy(i):
        peer = lax.rem(q + i, NCOL)
        return pltpu.make_async_remote_copy(
            src_ref=acts_ref.at[pl.ds(pl.multiple_of(peer * PIECE, PIECE), PIECE)],
            dst_ref=pieces.at[q],
            send_sem=a2a_s,
            recv_sem=a2a_r,
            device_id=at_col(i),
            device_id_type=MESH,
        )

    @pl.loop(1, NCOL)
    def _(i):
        piece_copy(i).start()

    for copy in loads:
        copy.wait()
    recv(pieces.at[pl.ds(0, NCOL - 1)], a2a_r)

    def peer_x(i):
        return {"col": (lax.rem(x + i, 4) * 4 + y) * 2 + core}

    def peer_y(i):
        return {"col": (x * 4 + lax.rem(y + i, 4)) * 2 + core}

    for k in range(STEPS):
        blocks[k, x, y, core] = pieces[order_ref[k]]
    for k in range(STEPS):
        mine = blocks.at[k, x, y, core]
        first = peer_x if k % 2 == 0 else peer_y
        for i in (1, 3, 2):
            send(mine, mine, line_s, line_r.at[k], first(i))

    def start_plane(k):
        recv(blocks.at[k, 0:3, 0, 0], line_r.at[k])
        mine = blocks.at[k, :, y, core] if k % 2 == 0 else blocks.at[k, x, :, core]
        second = peer_y if k % 2 == 0 else peer_x
        for i in (1, 3, 2):
            send(mine, mine, plane_s, plane_r.at[k], second(i))

    def start_twin(k):
        recv(blocks.at[k, 0:3, :, 0], plane_r.at[k])
        mine = blocks.at[k, :, :, core]
        send(mine, mine, twin_s, twin_r.at[k], {"col": q + 1 - 2 * core})

    start_plane(0)
    start_plane(1)
    start_twin(0)

    scale = math.sqrt(CH)
    eta_unit = float(CH) / float(TOKENS)
    thresh_unit = math.sqrt(D)
    for k in range(STEPS):
        recv(blocks.at[k, :, :, 0], twin_r.at[k])
        block_acts = blocks[k].reshape(TOKENS // NZ, BLOCK)
        lowered = out_ref[...].astype(BF16)
        grad[...] = lax.dot_general(
            block_acts, lowered, (((0,), (0,)), ((), ())), preferred_element_type=F32
        )

        def partial(a, b):
            owner = lax.rem(z + FAR[a] + near[b] + 2 * NZ, NZ)
            return fold(grad[pl.ds(pl.multiple_of(owner * ROWS, 8), ROWS), :])

        for a in FAR_ORDER + (0,):
            for b in (1, 2, 3):
                near_out[k, a, b - 1] = partial(a, b).astype(BF16)
                send(near_out.at[k, a, b - 1], near_in.at[k, a, b - 1], near_s, near_r.at[k, a], at_z(near[b]))
        if k + 2 < STEPS:
            start_plane(k + 2)
        if k + 1 < STEPS:
            start_twin(k + 1)
        for a in FAR_ORDER + (0,):
            total = partial(a, 0)
            recv(near_in.at[k, a], near_r.at[k, a])
            for b in range(3):
                total = total + near_in[k, a, b].astype(F32)
            if a:
                far_out[k, a - 1] = total.astype(BF16)
                send(far_out.at[k, a - 1], far_in.at[k, a - 1], far_s, far_r.at[k], at_z(FAR[a]))
        recv(far_in.at[k], far_r.at[k])
        for a in range(3):
            total = total + far_in[k, a].astype(F32)
        mean_grad = jnp.concatenate([total[:ROWS], total[ROWS:]], axis=1) / scale

        which = order_ref[k]
        current = weights_ref[which].astype(F32)
        for j in range(k):
            current = jnp.where(order_ref[j] == which, fresh_ref[j], current)
        shifted = current - (rate_ref[which] * eta_unit) * mean_grad
        square = shifted * shifted
        square = square[:, :HALF] + square[:, HALF:]
        square = jnp.concatenate([square, jnp.zeros((HALF - ROWS, HALF), F32)], axis=0)
        sums[k, q] = jnp.sum(square.T, axis=0, keepdims=True)

        def sum_copy(i):
            return pltpu.make_async_remote_copy(
                src_ref=sums.at[k, q],
                dst_ref=sums.at[k, q],
                send_sem=sum_s,
                recv_sem=sum_r.at[k],
                device_id=at_col(i),
                device_id_type=MESH,
            )

        @pl.loop(1, NCOL)
        def _(i):
            sum_copy(i).start()

        recv(sums.at[k, pl.ds(0, NCOL - 1)], sum_r.at[k])
        whole = jnp.sum(sums[k], axis=0)
        limit = penalty_ref[which] * thresh_unit
        factor = jnp.maximum(0.0, 1.0 - limit / jnp.sqrt(whole + 1e-06))
        factor = jnp.broadcast_to(factor, (HALF, HALF)).T[:ROWS]
        fresh = jnp.concatenate([factor, factor], axis=1) * shifted
        fresh_ref[k] = fresh

        gathered[k, 0, 0] = fold(fresh - current).astype(BF16)
        mine = gathered.at[k, 0, 0]
        for a in FAR_ORDER:
            send(mine, gathered.at[k, a, 0], gf_s, gf_r.at[k, a - 1], at_z(FAR[a]))
        for a in (0, 1, 2, 3):
            if a:
                recv(gathered.at[k, a, 0], gf_r.at[k, a - 1])
            for b in (1, 2, 3):
                send(gathered.at[k, a, 0], gathered.at[k, a, b], gn_s, gn_r.at[k], at_z(near[b]))
        recv(gathered.at[k, :, 1:4], gn_r.at[k])
        for a in range(4):
            for b in range(4):
                source = lax.rem(z - FAR[a] - near[b] + 2 * NZ, NZ)
                change[pl.ds(pl.multiple_of(source * ROWS, 8), ROWS), :] = unfold(gathered[k, a, b])
        out_ref[...] = out_ref[...] + (
            jnp.dot(block_acts, change[...].astype(BF16), preferred_element_type=F32) / scale
        )
    sent(pieces.at[pl.ds(0, NCOL - 1)], a2a_s)
    sent(blocks.at[:, 0:3, 0, 0], line_s)
    sent(blocks.at[:, 0:3, :, 0], plane_s)
    sent(blocks.at[:, :, :, 0], twin_s)
    sent(near_out, near_s)
    sent(far_out, far_s)
    sent(sums.at[:, pl.ds(0, NCOL - 1)], sum_s)
    sent(gathered.at[:, 1:4, 0], gf_s)
    sent(gathered.at[:, :, 1:4], gn_s)


def place_kernel(order_ref, weights_ref, fresh_ref, out_ref):
    out_ref[...] = weights_ref[...].astype(F32)
    for k in range(STEPS):
        out_ref[order_ref[k]] = fresh_ref[k]


def body(acts, residual, weights, order, rate, penalty):
    smem = pl.BlockSpec(memory_space=pltpu.SMEM)
    vmem = pl.BlockSpec(memory_space=pltpu.VMEM)
    hbm = pl.BlockSpec(memory_space=pl.ANY)
    one = pltpu.SemaphoreType.DMA(())
    sems = pltpu.SemaphoreType.DMA
    fresh, resid = pl.pallas_call(
        kernel,
        out_shape=(
            jax.ShapeDtypeStruct((STEPS, ROWS, COLS), F32),
            jax.ShapeDtypeStruct(residual.shape, F32),
        ),
        in_specs=[hbm] * 6,
        out_specs=(vmem, vmem),
        scratch_shapes=[
            pltpu.SMEM((STEPS,), jnp.int32),
            pltpu.SMEM((NBLK,), F32),
            pltpu.SMEM((NBLK,), F32),
            pltpu.VMEM(weights.shape, BF16),
            pltpu.VMEM((NCOL, PIECE, BLOCK), BF16),
            pltpu.VMEM((STEPS, 4, 4, 2, PIECE, BLOCK), BF16),
            pltpu.VMEM((BLOCK, COLS), F32),
            pltpu.VMEM((STEPS, 4, 3) + CHUNK, BF16),
            pltpu.VMEM((STEPS, 4, 3) + CHUNK, BF16),
            pltpu.VMEM((STEPS, 3) + CHUNK, BF16),
            pltpu.VMEM((STEPS, 3) + CHUNK, BF16),
            pltpu.VMEM((STEPS, NCOL, 1, HALF), F32),
            pltpu.VMEM((STEPS, 4, 4) + CHUNK, BF16),
            pltpu.VMEM((BLOCK, COLS), F32),
            sems((6,)),
            one, sems((STEPS,)), sems((STEPS,)), sems((STEPS,)), sems((STEPS, 4)),
            sems((STEPS,)), sems((STEPS,)), sems((STEPS, 3)), sems((STEPS,)),
            one, one, one, one, one, one, one, one, one,
        ],
        compiler_params=pltpu.CompilerParams(
            collective_id=0, has_side_effects=True, vmem_limit_bytes=62 * 1024 * 1024
        ),
        name="steps",
    )(order, rate, penalty, acts, residual, weights)
    pruned = pl.pallas_call(
        place_kernel,
        out_shape=jax.ShapeDtypeStruct(weights.shape, F32),
        in_specs=[smem, vmem, vmem],
        out_specs=vmem,
        compiler_params=pltpu.CompilerParams(vmem_limit_bytes=16 * 1024 * 1024),
        name="place",
    )(order, weights, fresh)
    return (pruned, resid)


def solution(mesh):
    in_specs = (P("tok", "col"), P("tok", "col"), P(None, "tok", "col"), P(), P(), P())
    out_specs = (P(None, "tok", "col"), P("tok", "col"))
    return jax.shard_map(body, mesh=mesh, in_specs=in_specs, out_specs=out_specs, check_vma=False)
```

time: 201 us -> 188 us (0.935)
  Pallas kernels: 192 us -> 185 us
  local copies, waits for them, and re-layouts: 6.15 us -> 1.74 us
    pallas_call x1, Pallas kernels: 190 us -> 183 us  [body(): pl.pallas_call(kernel, out_shape=(jax.ShapeDtypeStruct((STEPS, ROWS, COLS...]
    unnamed x13 -> x9, local copies, waits for them, and re-layouts: 6.15 us -> 1.74 us
where the time goes in v2:
time: 188 us; the launch traced here: 187 us
  Pallas kernels  185 us (98%)
    pallas_call x1, Pallas kernels, body(): pl.pallas_call(kernel, out_shape=(jax.ShapeDtypeStruct((STEPS, ROWS, COLS...  183 us

profile of v2, /device:TPU:1, one launch (start us, length us, event | category | flops | bytes accessed | tf_op | source)
XLA Modules:
  0.0 187.1 jit_solution(12970718531023744577)
XLA Ops:
  0.6 0.0 copy-start.2
  0.6 0.0 copy-start
  0.7 182.8 %steps.1 = (f32[4,56,256]{2,1,0:T(8,128)}, f32[512,256]{1,0:T(8,128)}) custom-call(s32[4]{0:T(128)} %order_ref.1, f32[32]{0:T(128)} %rate_hbm.1, f32[32]{0:T(128)} %penalty_hbm.1, bf16[512,896]{1,0:T(8,128)(2,1)} %acts_ref.1, f32[512,256]{1,0:T(8,128)} %resid_ref.1, bf16[32,56,256]{2,1,0:T(8,128)(2,1)} %weights_ref.1), custom_call_target="tpu_custom_call" | custom-call | tf_op jit(solution)/shard_map/steps/pallas_call | solution.py:255
  183.4 0.0 copy-done.2
  183.4 0.0 copy-done
  183.5 0.0 copy-start.1
  183.5 0.9 copy-done.1
  184.4 0.0 copy-start.3
  184.4 1.9 %place.1 = f32[32,56,256]{2,1,0:T(8,128)} custom-call(s32[4]{0:T(128)S(1)} %copy-done.2, bf16[32,56,256]{2,1,0:T(8,128)(2,1)S(1)} %copy-done, f32[4,56,256]{2,1,0:T(8,128)S(1)} %copy-done.1), custom_call_target="tpu_custom_call" | custom-call | tf_op jit(solution)/shard_map/place/pallas_call | solution.py:288
  186.3 0.0 copy-done.3
  186.3 0.8 copy.9
Async XLA Ops:
  0.6 182.8 %copy-start.2 = (s32[4]{0:T(128)S(1)}, s32[4]{0:T(128)}, u32[]{:S(2)}) copy-start(s32[4]{0:T(128)} %order_ref.1) | copy-start | bytes 52
  0.6 182.8 %copy-start = (bf16[32,56,256]{2,1,0:T(8,128)(2,1)S(1)}, bf16[32,56,256]{2,1,0:T(8,128)(2,1)}, u32[]{:S(2)}) copy-start(bf16[32,56,256]{2,1,0:T(8,128)(2,1)} %weights_ref.1) | copy-start | bytes 2752516
  183.5 0.9 copy-start.1
  184.4 1.9 %copy-start.3 = (f32[512,256]{1,0:T(8,128)S(1)}, f32[512,256]{1,0:T(8,128)}, u32[]{:S(2)}) copy-start(f32[512,256]{1,0:T(8,128)} %get-tuple-element.9) | copy-start | bytes 1572868

commit v3 on v2

v3 whole, which is shorter than its diff:
```python
import math

import jax
import jax.numpy as jnp
from jax import lax
from jax.experimental import pallas as pl
from jax.experimental.pallas import tpu as pltpu
from jax.sharding import PartitionSpec as P

D = 8192
CH = 28672
STEPS = 4
NBLK = 32
BLOCK = 896
TOKENS = 8192
NZ = 16
NCOL = 32
ROWS = BLOCK // NZ
COLS = D // NCOL
PIECE = TOKENS // NZ // NCOL
HALF = COLS // 2
CHUNK = (2 * ROWS, HALF)
FAR = (0, 3, -3, 6, -6)
FAR_ORDER = (3, 4, 1, 2)
NEAR = (0, 1, -1)
CUT = 48
SETS = STEPS + 2
TILES = BLOCK // HALF
PAIR = {(1, 0): 0, (2, 0): 1, (2, 1): 2, (3, 0): 3, (3, 1): 4, (3, 2): 5}
GRAM_COUNT = ((TILES + 1) // 2, (5 * TILES + 1) // 2)
GRAM_AT = (0, GRAM_COUNT[0])
GRAM_SPOT = (GRAM_COUNT[1], 0)
MESH = pl.DeviceIdType.MESH
F32 = jnp.float32
BF16 = jnp.bfloat16


def fold(rows):
    return jnp.concatenate([rows[:, :HALF], rows[:, HALF:]], axis=0)


def unfold(chunk):
    wide = chunk.astype(F32)
    return jnp.concatenate([wide[:ROWS], wide[ROWS:]], axis=1)


def kernel(
    order_hbm, rate_hbm, penalty_hbm, acts_ref, resid_ref, weights_hbm,
    fresh_ref, out_ref,
    order_ref, rate_ref, penalty_ref, weights_ref, lowered,
    pieces, blocks, source, near_out, near_in, across_out, across_in, near_sum, far_out, far_in, sums, gathered, opposite, change, delta,
    gram_in, gram,
    load_sems, a2a_r, line_r, plane_r, twin_r, near_r, across_r, far_r, sum_r, gf_r, gn_r, go_r, gram_r,
    a2a_s, line_s, plane_s, twin_s, near_s, across_s, far_s, sum_s, gf_s, gn_s, go_s, gram_s,
):
    z = lax.axis_index("tok")
    q = lax.axis_index("col")
    core = lax.rem(q, 2)
    y = lax.rem(q // 2, 4)
    x = q // 8
    spot = q // 2 + NCOL // 2 * core

    def at_z(offset):
        return {"tok": lax.rem(z + offset + 2 * NZ, NZ)}

    def at_col(i):
        return {"col": lax.rem(q + i, NCOL)}

    def remote(src, dst, ssem, rsem, where):
        return pltpu.make_async_remote_copy(
            src_ref=src, dst_ref=dst, send_sem=ssem, recv_sem=rsem, device_id=where, device_id_type=MESH
        )

    def send(src, dst, ssem, rsem, where):
        remote(src, dst, ssem, rsem, where).start()

    def recv(ref, sem):
        remote(ref, ref, a2a_s, sem, at_z(1)).wait_recv()

    def sent(ref, sem):
        remote(ref, ref, sem, a2a_r, at_z(1)).wait_send()

    own_rows = pl.ds(pl.multiple_of(q * PIECE, PIECE), PIECE)
    loads = [
        pltpu.make_async_copy(src, dst, load_sems.at[i])
        for i, (src, dst) in enumerate((
            (acts_ref.at[own_rows], pieces.at[q]),
            (order_hbm, order_ref),
            (rate_hbm, rate_ref),
            (penalty_hbm, penalty_ref),
            (resid_ref, out_ref),
            (weights_hbm, weights_ref),
        ))
    ]
    for copy in loads:
        copy.start()

    barrier = pltpu.get_barrier_semaphore()

    @pl.loop(1, NCOL)
    def _(i):
        pl.semaphore_signal(barrier, inc=1, device_id=at_col(i), device_id_type=MESH)

    for offset in (1, -1, 2, -2, 3, -3, 6, -6):
        pl.semaphore_signal(barrier, inc=1, device_id=at_z(offset), device_id_type=MESH)
    pl.semaphore_wait(barrier, NCOL - 1 + 8)

    @pl.loop(1, NCOL)
    def _(i):
        peer = lax.rem(q + i, NCOL)
        rows = pl.ds(pl.multiple_of(peer * PIECE, PIECE), PIECE)
        send(acts_ref.at[rows], pieces.at[q], a2a_s, a2a_r, at_col(i))

    for copy in loads:
        copy.wait()
    lowered[...] = out_ref[...].astype(BF16)
    recv(pieces.at[pl.ds(0, NCOL - 1)], a2a_r)

    def peer_x(i):
        return {"col": (lax.rem(x + i, 4) * 4 + y) * 2 + core}

    def peer_y(i):
        return {"col": (x * 4 + lax.rem(y + i, 4)) * 2 + core}

    for k in range(STEPS):
        blocks[k, x, y, core] = pieces[order_ref[k]]
    first_piece = blocks.at[0, x, y, core]

    @pl.loop(1, NCOL // 2)
    def _(i):
        send(first_piece, first_piece, line_s.at[0], line_r.at[0], {"col": lax.rem(q + 2 * i, NCOL)})

    for k in range(1, STEPS):
        mine = blocks.at[k, x, y, core]
        first = peer_x if k % 2 == 0 else peer_y
        for i in (1, 3, 2):
            send(mine, mine, line_s.at[1], line_r.at[k], first(i))

    def start_plane(k):
        recv(blocks.at[k, 0:3, 0, 0], line_r.at[k])
        mine = blocks.at[k, :, y, core] if k % 2 == 0 else blocks.at[k, x, :, core]
        second = peer_y if k % 2 == 0 else peer_x
        for i in (1, 3, 2):
            send(mine, mine, plane_s, plane_r.at[k], second(i))

    def start_twin(k):
        if k == 0:
            recv(pieces.at[pl.ds(0, NCOL // 2 - 1)], line_r.at[0])
        else:
            recv(blocks.at[k, 0:3, :, 0], plane_r.at[k])
        mine = blocks.at[k, :, :, core]
        send(mine, mine, twin_s, twin_r.at[k], {"col": q + 1 - 2 * core})

    def ready(k):
        recv(blocks.at[k, :, :, 0], twin_r.at[k])

    def block_acts(k):
        return blocks[k].reshape(TOKENS // NZ, BLOCK)

    def over_tokens(a, b):
        return lax.dot_general(a, b, (((0,), (0,)), ((), ())), preferred_element_type=F32)

    def partial(s, offset):
        owner = lax.rem(z + offset + 2 * NZ, NZ)
        return fold(source[s, pl.ds(pl.multiple_of(owner * ROWS, 8), ROWS), :])

    def sum_kind(s):
        return max(0, s - 3)

    halves = ((pl.ds(0, CUT), 2), (pl.ds(CUT, CHUNK[0] - CUT), -2))

    def sum_start(s):
        kind = sum_kind(s)
        across_out[s] = partial(s, NZ // 2).astype(BF16)
        for i, (rows, offset) in enumerate(halves):
            send(
                across_out.at[s, rows], across_in.at[s, rows], across_s.at[kind], across_r.at[s, i], at_z(offset)
            )
        for a in FAR_ORDER + (0,):
            for b in (1, 2):
                near_out[s, a, b - 1] = partial(s, FAR[a] + NEAR[b]).astype(BF16)
                send(
                    near_out.at[s, a, b - 1], near_in.at[s, a, b - 1],
                    near_s.at[kind], near_r.at[s, a], at_z(NEAR[b]),
                )

    def sum_middle(s):
        kind = sum_kind(s)
        for a in FAR_ORDER + (0,):
            total = partial(s, FAR[a])
            recv(near_in.at[s, a], near_r.at[s, a])
            for b in range(2):
                total = total + near_in[s, a, b].astype(F32)
            if a == 3:
                recv(across_in.at[s, 0:CUT], across_r.at[s, 0])
                top = total[:CUT] + across_in[s, 0:CUT].astype(F32)
                total = jnp.concatenate([top, total[CUT:]], axis=0)
            if a == 4:
                recv(across_in.at[s, CUT : CHUNK[0]], across_r.at[s, 1])
                low = total[CUT:] + across_in[s, CUT : CHUNK[0]].astype(F32)
                total = jnp.concatenate([total[:CUT], low], axis=0)
            if a:
                far_out[s, a - 1] = total.astype(BF16)
                send(far_out.at[s, a - 1], far_in.at[s, a - 1], far_s.at[kind], far_r.at[s], at_z(FAR[a]))
            else:
                near_sum[s] = total

    def sum_end(s):
        recv(far_in.at[s], far_r.at[s])
        total = near_sum[s]
        for a in range(4):
            total = total + far_in[s, a].astype(F32)
        return total

    def gradient(k):
        source[k] = over_tokens(block_acts(k), lowered[...])
        sum_start(k)

    def tile(k, t):
        lanes = pl.ds(pl.multiple_of(t * HALF, HALF), HALF)
        return blocks[k, :, :, :, :, lanes].reshape(TOKENS // NZ, HALF)

    def gram_first():
        for h in range(2):
            source[4, :, h * HALF : (h + 1) * HALF] = over_tokens(block_acts(1), tile(0, lax.rem(2 * (spot - GRAM_SPOT[0]) + h, TILES)))
        sum_start(4)

    def gram_rest():
        for h in range(2):
            item = lax.rem(2 * spot + h, 5 * TILES)
            pair = item // TILES
            later = (pair + 1) // 3
            source[5, :, h * HALF : (h + 1) * HALF] = over_tokens(
                block_acts(2 + later), tile(pair - 2 * later, lax.rem(item, TILES))
            )
        sum_start(5)

    def gram_send(kind):
        at = GRAM_AT[kind] + spot - GRAM_SPOT[kind]
        gram_in[at] = sum_end(4 + kind).astype(BF16)

        @pl.loop(1, NCOL)
        def _(i):
            send(gram_in.at[at], gram_in.at[at], gram_s.at[kind], gram_r.at[kind], at_col(i))

    def gram_recv(kind):
        count = GRAM_COUNT[kind]

        @pl.when(has_gram[kind])
        def _():
            recv(gram_in.at[pl.ds(0, count - 1)], gram_r.at[kind])

        @pl.when(jnp.logical_not(has_gram[kind]))
        def _():
            recv(gram_in.at[pl.ds(0, count)], gram_r.at[kind])

        for item in range((1, 5)[kind] * TILES):
            chunk = gram_in[GRAM_AT[kind] + item // 2].astype(F32)
            at = ROWS * (item % 2)
            lane = HALF * (item % TILES)
            gram[kind + item // TILES, :, lane : lane + HALF] = chunk[at : at + ROWS]

    def correction(k, j):
        return jnp.dot(gram[PAIR[k, j]].astype(BF16), delta[j], preferred_element_type=F32)

    scale = math.sqrt(CH)
    eta_unit = float(CH) / float(TOKENS)
    thresh_unit = math.sqrt(D)

    def shift(k, corrections):
        total = sum_end(k)
        whole = jnp.concatenate([total[:ROWS], total[ROWS:]], axis=1)
        for value in corrections:
            whole = whole + value / scale
        which = order_ref[k]
        current = weights_ref[which].astype(F32)
        for j in range(k):
            current = jnp.where(order_ref[j] == which, fresh_ref[j], current)
        shifted = current - (rate_ref[which] * eta_unit) * (whole / scale)
        square = shifted * shifted
        square = square[:, :HALF] + square[:, HALF:]
        square = jnp.concatenate([square, jnp.zeros((HALF - ROWS, HALF), F32)], axis=0)
        sums[k, q] = jnp.sum(square.T, axis=0, keepdims=True)

        @pl.loop(1, NCOL)
        def _(i):
            send(sums.at[k, q], sums.at[k, q], sum_s, sum_r.at[k], at_col(i))

        return current, shifted

    def shrink(k, current, shifted, meanwhile=None):
        recv(sums.at[k, pl.ds(0, NCOL - 1)], sum_r.at[k])
        whole = jnp.sum(sums[k], axis=0)
        limit = penalty_ref[order_ref[k]] * thresh_unit
        factor = jnp.maximum(0.0, 1.0 - limit / jnp.sqrt(whole + 1e-06))
        factor = jnp.broadcast_to(factor, (HALF, HALF)).T[:ROWS]
        fresh = jnp.concatenate([factor, factor], axis=1) * shifted
        fresh_ref[k] = fresh
        gathered[k, 0, 0] = fold(fresh - current).astype(BF16)
        for a in FAR_ORDER:
            send(gathered.at[k, 0, 0], gathered.at[k, a, 0], gf_s, gf_r.at[k, a - 1], at_z(FAR[a]))
        for b in (1, 2):
            send(gathered.at[k, 0, 0], gathered.at[k, 0, b], gn_s, gn_r.at[k], at_z(NEAR[b]))
        if meanwhile is not None:
            meanwhile()
        for a in range(1, 5):
            recv(gathered.at[k, a, 0], gf_r.at[k, a - 1])
            if a >= 3:
                rows, offset = halves[a - 3]
                send(gathered.at[k, a, 0, rows], opposite.at[k, rows], go_s, go_r.at[k], at_z(offset))
            for b in (1, 2):
                send(gathered.at[k, a, 0], gathered.at[k, a, b], gn_s, gn_r.at[k], at_z(NEAR[b]))

    def collect(k):
        def put(offset, chunk):
            owner = lax.rem(z - offset + 2 * NZ, NZ)
            change[pl.ds(pl.multiple_of(owner * ROWS, 8), ROWS), :] = unfold(chunk)

        for a in range(5):
            put(FAR[a], gathered[k, a, 0])
        recv(gathered.at[k, :, 1:3], gn_r.at[k])
        recv(opposite.at[k], go_r.at[k])
        for a in range(5):
            for b in (1, 2):
                put(FAR[a] + NEAR[b], gathered[k, a, b])
        put(NZ // 2, opposite[k])
        delta[k] = change[...].astype(BF16)

    def update(k):
        out_ref[...] = out_ref[...] + (
            jnp.dot(block_acts(k), delta[k], preferred_element_type=F32) / scale
        )

    has_gram = [
        (spot >= GRAM_SPOT[kind]) & (spot < GRAM_SPOT[kind] + GRAM_COUNT[kind]) for kind in range(2)
    ]

    start_plane(1)
    start_twin(0)
    ready(0)
    gradient(0)
    start_plane(2)
    start_plane(3)
    start_twin(1)
    sum_middle(0)
    ready(1)
    gradient(1)
    pl.when(has_gram[0])(gram_first)
    start_twin(2)
    start_twin(3)

    current, shifted = shift(0, [])
    sum_middle(1)
    pl.when(has_gram[0])(lambda: sum_middle(4))
    shrink(0, current, shifted, lambda: pl.when(has_gram[0])(lambda: gram_send(0)))
    ready(2)
    gradient(2)
    ready(3)
    pl.when(has_gram[1])(gram_rest)
    collect(0)
    gram_recv(0)

    current, shifted = shift(1, [correction(1, 0)])
    update(0)
    sum_middle(2)
    pl.when(has_gram[1])(lambda: sum_middle(5))
    shrink(1, current, shifted, lambda: pl.when(has_gram[1])(lambda: gram_send(1)))
    gradient(3)
    collect(1)
    gram_recv(1)

    current, shifted = shift(2, [correction(2, 0), correction(2, 1)])
    update(1)
    early = [correction(3, 0), correction(3, 1)]
    sum_middle(3)
    shrink(2, current, shifted)
    collect(2)

    current, shifted = shift(3, early + [correction(3, 2)])
    update(2)
    shrink(3, current, shifted)
    collect(3)
    update(3)

    sent(pieces.at[pl.ds(0, NCOL - 1)], a2a_s)
    sent(pieces.at[pl.ds(0, NCOL // 2 - 1)], line_s.at[0])
    sent(blocks.at[1:STEPS, 0:3, 0, 0], line_s.at[1])
    sent(blocks.at[1:STEPS, 0:3, :, 0], plane_s)
    sent(blocks.at[:, :, :, 0], twin_s)
    sent(near_out.at[0:STEPS], near_s.at[0])
    sent(across_out.at[0:STEPS], across_s.at[0])
    sent(far_out.at[0:STEPS], far_s.at[0])
    sent(sums.at[:, pl.ds(0, NCOL - 1)], sum_s)
    sent(gathered.at[:, 1:5, 0], gf_s)
    sent(gathered.at[:, :, 1:3], gn_s)
    sent(opposite, go_s)
    for kind in range(2):

        @pl.when(has_gram[kind])
        def _():
            sent(near_out.at[0], near_s.at[1 + kind])
            sent(across_out.at[0], across_s.at[1 + kind])
            sent(far_out.at[0], far_s.at[1 + kind])
            sent(gram_in.at[pl.ds(0, NCOL - 1)], gram_s.at[kind])


def place_kernel(order_ref, weights_ref, fresh_ref, out_ref):
    out_ref[...] = weights_ref[...].astype(F32)
    for k in range(STEPS):
        out_ref[order_ref[k]] = fresh_ref[k]


def body(acts, residual, weights, order, rate, penalty):
    smem = pl.BlockSpec(memory_space=pltpu.SMEM)
    vmem = pl.BlockSpec(memory_space=pltpu.VMEM)
    hbm = pl.BlockSpec(memory_space=pl.ANY)
    one = pltpu.SemaphoreType.DMA(())
    sems = pltpu.SemaphoreType.DMA
    fresh, resid = pl.pallas_call(
        kernel,
        out_shape=(
            jax.ShapeDtypeStruct((STEPS, ROWS, COLS), F32),
            jax.ShapeDtypeStruct(residual.shape, F32),
        ),
        in_specs=[hbm] * 6,
        out_specs=(vmem, vmem),
        scratch_shapes=[
            pltpu.SMEM((STEPS,), jnp.int32),
            pltpu.SMEM((NBLK,), F32),
            pltpu.SMEM((NBLK,), F32),
            pltpu.VMEM(weights.shape, BF16),
            pltpu.VMEM(residual.shape, BF16),
            pltpu.VMEM((NCOL, PIECE, BLOCK), BF16),
            pltpu.VMEM((STEPS, 4, 4, 2, PIECE, BLOCK), BF16),
            pltpu.VMEM((SETS, BLOCK, COLS), F32),
            pltpu.VMEM((SETS, 5, 2) + CHUNK, BF16),
            pltpu.VMEM((SETS, 5, 2) + CHUNK, BF16),
            pltpu.VMEM((SETS,) + CHUNK, BF16),
            pltpu.VMEM((SETS,) + CHUNK, BF16),
            pltpu.VMEM((SETS,) + CHUNK, F32),
            pltpu.VMEM((SETS, 4) + CHUNK, BF16),
            pltpu.VMEM((SETS, 4) + CHUNK, BF16),
            pltpu.VMEM((STEPS, NCOL, 1, HALF), F32),
            pltpu.VMEM((STEPS, 5, 3) + CHUNK, BF16),
            pltpu.VMEM((STEPS,) + CHUNK, BF16),
            pltpu.VMEM((BLOCK, COLS), F32),
            pltpu.VMEM((STEPS, BLOCK, COLS), BF16),
            pltpu.VMEM((NCOL,) + CHUNK, BF16),
            pltpu.VMEM((len(PAIR), ROWS, BLOCK), F32),
            sems((6,)),
            one, sems((STEPS,)), sems((STEPS,)), sems((STEPS,)), sems((SETS, 5)), sems((SETS, 2)),
            sems((SETS,)), sems((STEPS,)), sems((STEPS, 4)), sems((STEPS,)), sems((STEPS,)), sems((2,)),
            one, sems((2,)), one, one, sems((3,)), sems((3,)), sems((3,)), one, one, one, one, sems((2,)),
        ],
        compiler_params=pltpu.CompilerParams(
            collective_id=0, has_side_effects=True, vmem_limit_bytes=62 * 1024 * 1024
        ),
        name="steps",
    )(order, rate, penalty, acts, residual, weights)
    pruned = pl.pallas_call(
        place_kernel,
        out_shape=jax.ShapeDtypeStruct(weights.shape, F32),
        in_specs=[smem, vmem, vmem],
        out_specs=vmem,
        compiler_params=pltpu.CompilerParams(vmem_limit_bytes=16 * 1024 * 1024),
        name="place",
    )(order, weights, fresh)
    return (pruned, resid)


def solution(mesh):
    in_specs = (P("tok", "col"), P("tok", "col"), P(None, "tok", "col"), P(), P(), P())
    out_specs = (P(None, "tok", "col"), P("tok", "col"))
    return jax.shard_map(body, mesh=mesh, in_specs=in_specs, out_specs=out_specs, check_vma=False)
```

time: 188 us -> 157 us (0.84)
  Pallas kernels: 185 us -> 154 us
    pallas_call x1, Pallas kernels: 183 us -> 152 us  [body(): pl.pallas_call(kernel, out_shape=(jax.ShapeDtypeStruct((STEPS, ROWS, COLS...]
where the time goes in v3:
time: 157 us; the launch traced here: 156 us
  Pallas kernels  154 us (98%)
  local copies, waits for them, and re-layouts  1.74 us (1%)
    pallas_call x1, Pallas kernels, body(): pl.pallas_call(kernel, out_shape=(jax.ShapeDtypeStruct((STEPS, ROWS, COLS...  152 us

profile of v3, /device:TPU:1, one launch (start us, length us, event | category | flops | bytes accessed | tf_op | source)
XLA Modules:
  0.0 156.4 jit_solution(1015746395990775463)
XLA Ops:
  0.6 0.0 copy-start.2
  0.6 0.0 copy-start
  0.7 152.1 %steps.1 = (f32[4,56,256]{2,1,0:T(8,128)}, f32[512,256]{1,0:T(8,128)}) custom-call(s32[4]{0:T(128)} %order_ref.1, f32[32]{0:T(128)} %rate_hbm.1, f32[32]{0:T(128)} %penalty_hbm.1, bf16[512,896]{1,0:T(8,128)(2,1)} %acts_ref.1, f32[512,256]{1,0:T(8,128)} %resid_ref.1, bf16[32,56,256]{2,1,0:T(8,128)(2,1)} %weights_ref.1), custom_call_target="tpu_custom_call" | custom-call | tf_op jit(solution)/shard_map/steps/pallas_call | solution.py:419
  152.7 0.0 copy-done.2
  152.8 0.0 copy-done
  152.8 0.0 copy-start.1
  152.8 0.9 copy-done.1
  153.7 0.0 copy-start.3
  153.7 1.9 %place.1 = f32[32,56,256]{2,1,0:T(8,128)} custom-call(s32[4]{0:T(128)S(1)} %copy-done.2, bf16[32,56,256]{2,1,0:T(8,128)(2,1)S(1)} %copy-done, f32[4,56,256]{2,1,0:T(8,128)S(1)} %copy-done.1), custom_call_target="tpu_custom_call" | custom-call | tf_op jit(solution)/shard_map/place/pallas_call | solution.py:460
  155.6 0.0 copy-done.3
  155.6 0.8 copy.9
Async XLA Ops:
  0.6 152.1 %copy-start.2 = (s32[4]{0:T(128)S(1)}, s32[4]{0:T(128)}, u32[]{:S(2)}) copy-start(s32[4]{0:T(128)} %order_ref.1) | copy-start | bytes 52
  0.6 152.1 %copy-start = (bf16[32,56,256]{2,1,0:T(8,128)(2,1)S(1)}, bf16[32,56,256]{2,1,0:T(8,128)(2,1)}, u32[]{:S(2)}) copy-start(bf16[32,56,256]{2,1,0:T(8,128)(2,1)} %weights_ref.1) | copy-start | bytes 2752516
  152.8 0.9 copy-start.1
  153.7 1.9 %copy-start.3 = (f32[512,256]{1,0:T(8,128)S(1)}, f32[512,256]{1,0:T(8,128)}, u32[]{:S(2)}) copy-start(f32[512,256]{1,0:T(8,128)} %get-tuple-element.9) | copy-start | bytes 1572868

commit v4 on v3

--- a/solution.py
+++ b/solution.py
@@ -19,6 +19,7 @@
 COLS = D // NCOL
 PIECE = TOKENS // NZ // NCOL
 HALF = COLS // 2
+EARLY = (3,)
 CHUNK = (2 * ROWS, HALF)
 FAR = (0, 3, -3, 6, -6)
 FAR_ORDER = (3, 4, 1, 2)
@@ -48,10 +49,10 @@
     order_hbm, rate_hbm, penalty_hbm, acts_ref, resid_ref, weights_hbm,
     fresh_ref, out_ref,
     order_ref, rate_ref, penalty_ref, weights_ref, lowered,
-    pieces, blocks, source, near_out, near_in, across_out, across_in, near_sum, far_out, far_in, sums, gathered, opposite, change, delta,
+    pieces, blocks, source, near_out, near_in, across_out, across_in, near_sum, far_out, far_in, sums, gathered, opposite, change, delta, held, factors,
     gram_in, gram,
-    load_sems, a2a_r, line_r, plane_r, twin_r, near_r, across_r, far_r, sum_r, gf_r, gn_r, go_r, gram_r,
-    a2a_s, line_s, plane_s, twin_s, near_s, across_s, far_s, sum_s, gf_s, gn_s, go_s, gram_s,
+    load_sems, a2a_r, line_r, plane_r, twin_r, near_r, across_r, far_r, sum_r, gf_r, gn_r, go_r, gram_r, factor_r,
+    a2a_s, line_s, plane_s, twin_s, near_s, across_s, far_s, sum_s, gf_s, gn_s, go_s, gram_s, factor_s,
 ):
     z = lax.axis_index("tok")
     q = lax.axis_index("col")
@@ -101,9 +102,43 @@
     def _(i):
         pl.semaphore_signal(barrier, inc=1, device_id=at_col(i), device_id_type=MESH)
 
-    for offset in (1, -1, 2, -2, 3, -3, 6, -6):
-        pl.semaphore_signal(barrier, inc=1, device_id=at_z(offset), device_id_type=MESH)
-    pl.semaphore_wait(barrier, NCOL - 1 + 8)
+    @pl.loop(1, NZ)
+    def _(i):
+        pl.semaphore_signal(barrier, inc=1, device_id=at_z(i), device_id_type=MESH)
+
+    pl.semaphore_wait(barrier, NCOL - 1 + NZ - 1)
+
+    halves = ((pl.ds(0, CUT), 2), (pl.ds(CUT, CHUNK[0] - CUT), -2))
+
+    def gather_start(g, rows):
+        gathered[g, 0, 0] = fold(rows).astype(BF16)
+        for a in FAR_ORDER:
+            send(gathered.at[g, 0, 0], gathered.at[g, a, 0], gf_s, gf_r.at[g, a - 1], at_z(FAR[a]))
+        for b in (1, 2):
+            send(gathered.at[g, 0, 0], gathered.at[g, 0, b], gn_s, gn_r.at[g], at_z(NEAR[b]))
+
+    def gather_forward(g):
+        for a in range(1, 5):
+            recv(gathered.at[g, a, 0], gf_r.at[g, a - 1])
+            if a >= 3:
+                rows, offset = halves[a - 3]
+                send(gathered.at[g, a, 0, rows], opposite.at[g, rows], go_s, go_r.at[g], at_z(offset))
+            for b in (1, 2):
+                send(gathered.at[g, a, 0], gathered.at[g, a, b], gn_s, gn_r.at[g], at_z(NEAR[b]))
+
+    def gather_collect(g):
+        def put(offset, chunk):
+            owner = lax.rem(z - offset + 2 * NZ, NZ)
+            change[pl.ds(pl.multiple_of(owner * ROWS, 8), ROWS), :] = unfold(chunk)
+
+        for a in range(5):
+            put(FAR[a], gathered[g, a, 0])
+        recv(gathered.at[g, :, 1:3], gn_r.at[g])
+        recv(opposite.at[g], go_r.at[g])
+        for a in range(5):
+            for b in (1, 2):
+                put(FAR[a] + NEAR[b], gathered[g, a, b])
+        put(NZ // 2, opposite[g])
 
     @pl.loop(1, NCOL)
     def _(i):
@@ -114,6 +149,8 @@
     for copy in loads:
         copy.wait()
     lowered[...] = out_ref[...].astype(BF16)
+    for k in EARLY:
+        gather_start(STEPS + EARLY.index(k), weights_ref[order_ref[k]].astype(F32))
     recv(pieces.at[pl.ds(0, NCOL - 1)], a2a_r)
 
     def peer_x(i):
@@ -166,8 +203,6 @@
 
     def sum_kind(s):
         return max(0, s - 3)
-
-    halves = ((pl.ds(0, CUT), 2), (pl.ds(CUT, CHUNK[0] - CUT), -2))
 
     def sum_start(s):
         kind = sum_kind(s)
@@ -286,6 +321,8 @@
         def _(i):
             send(sums.at[k, q], sums.at[k, q], sum_s, sum_r.at[k], at_col(i))
 
+        if k in EARLY:
+            gather_start(k, shifted)
         return current, shifted
 
     def shrink(k, current, shifted, meanwhile=None):
@@ -293,38 +330,38 @@
         whole = jnp.sum(sums[k], axis=0)
         limit = penalty_ref[order_ref[k]] * thresh_unit
         factor = jnp.maximum(0.0, 1.0 - limit / jnp.sqrt(whole + 1e-06))
-        factor = jnp.broadcast_to(factor, (HALF, HALF)).T[:ROWS]
+        row = factor
+        factor = jnp.broadcast_to(row, (HALF, HALF)).T[:ROWS]
         fresh = jnp.concatenate([factor, factor], axis=1) * shifted
         fresh_ref[k] = fresh
-        gathered[k, 0, 0] = fold(fresh - current).astype(BF16)
-        for a in FAR_ORDER:
-            send(gathered.at[k, 0, 0], gathered.at[k, a, 0], gf_s, gf_r.at[k, a - 1], at_z(FAR[a]))
-        for b in (1, 2):
-            send(gathered.at[k, 0, 0], gathered.at[k, 0, b], gn_s, gn_r.at[k], at_z(NEAR[b]))
+        if k in EARLY:
+            factors[k, z] = row
+
+            @pl.loop(1, NZ)
+            def _(i):
+                send(factors.at[k, z], factors.at[k, z], factor_s, factor_r.at[k], at_z(i))
+
+        else:
+            gather_start(k, fresh - current)
         if meanwhile is not None:
             meanwhile()
-        for a in range(1, 5):
-            recv(gathered.at[k, a, 0], gf_r.at[k, a - 1])
-            if a >= 3:
-                rows, offset = halves[a - 3]
-                send(gathered.at[k, a, 0, rows], opposite.at[k, rows], go_s, go_r.at[k], at_z(offset))
-            for b in (1, 2):
-                send(gathered.at[k, a, 0], gathered.at[k, a, b], gn_s, gn_r.at[k], at_z(NEAR[b]))
+        gather_forward(k)
 
     def collect(k):
-        def put(offset, chunk):
-            owner = lax.rem(z - offset + 2 * NZ, NZ)
-            change[pl.ds(pl.multiple_of(owner * ROWS, 8), ROWS), :] = unfold(chunk)
-
-        for a in range(5):
-            put(FAR[a], gathered[k, a, 0])
-        recv(gathered.at[k, :, 1:3], gn_r.at[k])
-        recv(opposite.at[k], go_r.at[k])
-        for a in range(5):
-            for b in (1, 2):
-                put(FAR[a] + NEAR[b], gathered[k, a, b])
-        put(NZ // 2, opposite[k])
-        delta[k] = change[...].astype(BF16)
+        gather_collect(k)
+        if k in EARLY:
+            recv(factors.at[k, pl.ds(0, NZ - 1)], factor_r.at[k])
+            table = jnp.concatenate([factors[k, j] for j in range(NZ)] + [jnp.zeros((HALF - NZ, HALF), F32)], axis=0).T
+            for j in range(NZ):
+                rows = slice(j * ROWS, (j + 1) * ROWS)
+                change[rows, :] = change[rows, :] * table[:ROWS, j : j + 1]
+            value = change[...] - held[k].astype(F32)
+            for j in range(k):
+                same = jnp.where(order_ref[j] == order_ref[k], 1.0, 0.0)
+                value = value - same * delta[j].astype(F32)
+            delta[k] = value.astype(BF16)
+        else:
+            delta[k] = change[...].astype(BF16)
 
     def update(k):
         out_ref[...] = out_ref[...] + (
@@ -335,6 +372,8 @@
         (spot >= GRAM_SPOT[kind]) & (spot < GRAM_SPOT[kind] + GRAM_COUNT[kind]) for kind in range(2)
     ]
 
+    for k in EARLY:
+        gather_forward(STEPS + EARLY.index(k))
     start_plane(1)
     start_twin(0)
     ready(0)
@@ -344,27 +383,35 @@
     start_twin(1)
     sum_middle(0)
     ready(1)
+    pl.when(has_gram[0])(gram_first)
     gradient(1)
-    pl.when(has_gram[0])(gram_first)
     start_twin(2)
     start_twin(3)
 
+    for k in EARLY:
+        gather_collect(STEPS + EARLY.index(k))
+        held[k] = change[...].astype(BF16)
+
     current, shifted = shift(0, [])
+    pl.when(has_gram[0])(lambda: sum_middle(4))
     sum_middle(1)
-    pl.when(has_gram[0])(lambda: sum_middle(4))
     shrink(0, current, shifted, lambda: pl.when(has_gram[0])(lambda: gram_send(0)))
     ready(2)
-    gradient(2)
     ready(3)
     pl.when(has_gram[1])(gram_rest)
+    gradient(2)
     collect(0)
     gram_recv(0)
 
     current, shifted = shift(1, [correction(1, 0)])
     update(0)
-    sum_middle(2)
     pl.when(has_gram[1])(lambda: sum_middle(5))
-    shrink(1, current, shifted, lambda: pl.when(has_gram[1])(lambda: gram_send(1)))
+
+    def beside():
+        pl.when(has_gram[1])(lambda: gram_send(1))
+        sum_middle(2)
+
+    shrink(1, current, shifted, beside)
     gradient(3)
     collect(1)
     gram_recv(1)
@@ -394,6 +441,7 @@
     sent(gathered.at[:, 1:5, 0], gf_s)
     sent(gathered.at[:, :, 1:3], gn_s)
     sent(opposite, go_s)
+    sent(factors.at[0 : len(EARLY), pl.ds(0, NZ - 1)], factor_s)
     for kind in range(2):
 
         @pl.when(has_gram[kind])
@@ -441,16 +489,19 @@
             pltpu.VMEM((SETS, 4) + CHUNK, BF16),
             pltpu.VMEM((SETS, 4) + CHUNK, BF16),
             pltpu.VMEM((STEPS, NCOL, 1, HALF), F32),
-            pltpu.VMEM((STEPS, 5, 3) + CHUNK, BF16),
-            pltpu.VMEM((STEPS,) + CHUNK, BF16),
+            pltpu.VMEM((STEPS + len(EARLY), 5, 3) + CHUNK, BF16),
+            pltpu.VMEM((STEPS + len(EARLY),) + CHUNK, BF16),
             pltpu.VMEM((BLOCK, COLS), F32),
             pltpu.VMEM((STEPS, BLOCK, COLS), BF16),
+            pltpu.VMEM((STEPS, BLOCK, COLS), BF16),
+            pltpu.VMEM((STEPS, NZ, 1, HALF), F32),
             pltpu.VMEM((NCOL,) + CHUNK, BF16),
             pltpu.VMEM((len(PAIR), ROWS, BLOCK), F32),
             sems((6,)),
             one, sems((STEPS,)), sems((STEPS,)), sems((STEPS,)), sems((SETS, 5)), sems((SETS, 2)),
-            sems((SETS,)), sems((STEPS,)), sems((STEPS, 4)), sems((STEPS,)), sems((STEPS,)), sems((2,)),
-            one, sems((2,)), one, one, sems((3,)), sems((3,)), sems((3,)), one, one, one, one, sems((2,)),
+            sems((SETS,)), sems((STEPS,)),
+            sems((STEPS + len(EARLY), 4)), sems((STEPS + len(EARLY),)), sems((STEPS + len(EARLY),)), sems((2,)), sems((STEPS,)),
+            one, sems((2,)), one, one, sems((3,)), sems((3,)), sems((3,)), one, one, one, one, sems((2,)), one,
         ],
         compiler_params=pltpu.CompilerParams(
             collective_id=0, has_side_effects=True, vmem_limit_bytes=62 * 1024 * 1024

time: 157 us -> 146 us (0.930)
  Pallas kernels: 154 us -> 143 us
    pallas_call x1, Pallas kernels: 152 us -> 141 us  [body(): pl.pallas_call(kernel, out_shape=(jax.ShapeDtypeStruct((STEPS, ROWS, COLS...]
where the time goes in v4:
time: 146 us; the launch traced here: 145 us
  Pallas kernels  143 us (98%)
  local copies, waits for them, and re-layouts  1.74 us (1%)
    pallas_call x1, Pallas kernels, body(): pl.pallas_call(kernel, out_shape=(jax.ShapeDtypeStruct((STEPS, ROWS, COLS...  141 us

profile of v4, /device:TPU:1, one launch (start us, length us, event | category | flops | bytes accessed | tf_op | source)
XLA Modules:
  0.0 145.5 jit_solution(742345643604944451)
XLA Ops:
  0.6 0.0 copy-start.2
  0.6 0.0 copy-start
  0.7 141.2 %steps.1 = (f32[4,56,256]{2,1,0:T(8,128)}, f32[512,256]{1,0:T(8,128)}) custom-call(s32[4]{0:T(128)} %order_ref.1, f32[32]{0:T(128)} %rate_hbm.1, f32[32]{0:T(128)} %penalty_hbm.1, bf16[512,896]{1,0:T(8,128)(2,1)} %acts_ref.1, f32[512,256]{1,0:T(8,128)} %resid_ref.1, bf16[32,56,256]{2,1,0:T(8,128)(2,1)} %weights_ref.1), custom_call_target="tpu_custom_call" | custom-call | tf_op jit(solution)/shard_map/steps/pallas_call | solution.py:467
  141.8 0.0 copy-done.2
  141.8 0.0 copy-done
  141.8 0.0 copy-start.1
  141.8 0.9 copy-done.1
  142.8 0.0 copy-start.3
  142.8 1.9 %place.1 = f32[32,56,256]{2,1,0:T(8,128)} custom-call(s32[4]{0:T(128)S(1)} %copy-done.2, bf16[32,56,256]{2,1,0:T(8,128)(2,1)S(1)} %copy-done, f32[4,56,256]{2,1,0:T(8,128)S(1)} %copy-done.1), custom_call_target="tpu_custom_call" | custom-call | tf_op jit(solution)/shard_map/place/pallas_call | solution.py:511
  144.7 0.0 copy-done.3
  144.7 0.8 copy.9
Async XLA Ops:
  0.6 141.2 %copy-start.2 = (s32[4]{0:T(128)S(1)}, s32[4]{0:T(128)}, u32[]{:S(2)}) copy-start(s32[4]{0:T(128)} %order_ref.1) | copy-start | bytes 52
  0.6 141.2 %copy-start = (bf16[32,56,256]{2,1,0:T(8,128)(2,1)S(1)}, bf16[32,56,256]{2,1,0:T(8,128)(2,1)}, u32[]{:S(2)}) copy-start(bf16[32,56,256]{2,1,0:T(8,128)(2,1)} %weights_ref.1) | copy-start | bytes 2752516
  141.8 0.9 copy-start.1
  142.8 1.9 %copy-start.3 = (f32[512,256]{1,0:T(8,128)S(1)}, f32[512,256]{1,0:T(8,128)}, u32[]{:S(2)}) copy-start(f32[512,256]{1,0:T(8,128)} %get-tuple-element.9) | copy-start | bytes 1572868

commit v5 on v4

--- a/solution.py
+++ b/solution.py
@@ -67,6 +67,16 @@
     def at_col(i):
         return {"col": lax.rem(q + i, NCOL)}
 
+    def for_columns(act):
+        @pl.loop(0, NCOL - 1)
+        def _(j):
+            act(1 + lax.rem(j + NCOL // 2 - 1, NCOL - 1))
+
+    def for_z(act):
+        @pl.loop(0, NZ - 1)
+        def _(j):
+            act(NZ // 2 + ((j + 1) // 2) * (1 - 2 * lax.rem(j, 2)))
+
     def remote(src, dst, ssem, rsem, where):
         return pltpu.make_async_remote_copy(
             src_ref=src, dst_ref=dst, send_sem=ssem, recv_sem=rsem, device_id=where, device_id_type=MESH
@@ -98,14 +108,8 @@
 
     barrier = pltpu.get_barrier_semaphore()
 
-    @pl.loop(1, NCOL)
-    def _(i):
-        pl.semaphore_signal(barrier, inc=1, device_id=at_col(i), device_id_type=MESH)
-
-    @pl.loop(1, NZ)
-    def _(i):
-        pl.semaphore_signal(barrier, inc=1, device_id=at_z(i), device_id_type=MESH)
-
+    for_z(lambda i: pl.semaphore_signal(barrier, inc=1, device_id=at_z(i), device_id_type=MESH))
+    for_columns(lambda i: pl.semaphore_signal(barrier, inc=1, device_id=at_col(i), device_id_type=MESH))
     pl.semaphore_wait(barrier, NCOL - 1 + NZ - 1)
 
     halves = ((pl.ds(0, CUT), 2), (pl.ds(CUT, CHUNK[0] - CUT), -2))
@@ -140,11 +144,12 @@
                 put(FAR[a] + NEAR[b], gathered[g, a, b])
         put(NZ // 2, opposite[g])
 
-    @pl.loop(1, NCOL)
-    def _(i):
+    def send_piece(i):
         peer = lax.rem(q + i, NCOL)
         rows = pl.ds(pl.multiple_of(peer * PIECE, PIECE), PIECE)
         send(acts_ref.at[rows], pieces.at[q], a2a_s, a2a_r, at_col(i))
+
+    for_columns(send_piece)
 
     for copy in loads:
         copy.wait()
@@ -163,8 +168,9 @@
         blocks[k, x, y, core] = pieces[order_ref[k]]
     first_piece = blocks.at[0, x, y, core]
 
-    @pl.loop(1, NCOL // 2)
-    def _(i):
+    @pl.loop(0, NCOL // 2 - 1)
+    def _(j):
+        i = 1 + lax.rem(j + NCOL // 4 - 1, NCOL // 2 - 1)
         send(first_piece, first_piece, line_s.at[0], line_r.at[0], {"col": lax.rem(q + 2 * i, NCOL)})
 
     for k in range(1, STEPS):
@@ -274,9 +280,9 @@
         at = GRAM_AT[kind] + spot - GRAM_SPOT[kind]
         gram_in[at] = sum_end(4 + kind).astype(BF16)
 
-        @pl.loop(1, NCOL)
-        def _(i):
-            send(gram_in.at[at], gram_in.at[at], gram_s.at[kind], gram_r.at[kind], at_col(i))
+        for_columns(
+            lambda i: send(gram_in.at[at], gram_in.at[at], gram_s.at[kind], gram_r.at[kind], at_col(i))
+        )
 
     def gram_recv(kind):
         count = GRAM_COUNT[kind]
@@ -317,9 +323,7 @@
         square = jnp.concatenate([square, jnp.zeros((HALF - ROWS, HALF), F32)], axis=0)
         sums[k, q] = jnp.sum(square.T, axis=0, keepdims=True)
 
-        @pl.loop(1, NCOL)
-        def _(i):
-            send(sums.at[k, q], sums.at[k, q], sum_s, sum_r.at[k], at_col(i))
+        for_columns(lambda i: send(sums.at[k, q], sums.at[k, q], sum_s, sum_r.at[k], at_col(i)))
 
         if k in EARLY:
             gather_start(k, shifted)
@@ -337,9 +341,7 @@
         if k in EARLY:
             factors[k, z] = row
 
-            @pl.loop(1, NZ)
-            def _(i):
-                send(factors.at[k, z], factors.at[k, z], factor_s, factor_r.at[k], at_z(i))
+            for_z(lambda i: send(factors.at[k, z], factors.at[k, z], factor_s, factor_r.at[k], at_z(i)))
 
         else:
             gather_start(k, fresh - current)

time: 146 us -> 145 us (level)
  Pallas kernels: 143 us -> 141 us
    pallas_call x1, Pallas kernels: 141 us -> 139 us  [body(): pl.pallas_call(kernel, out_shape=(jax.ShapeDtypeStruct((STEPS, ROWS, COLS...]
where the time goes in v5:
time: 145 us; the launch traced here: 144 us
  Pallas kernels  141 us (97%)
  local copies, waits for them, and re-layouts  1.74 us (1%)
    pallas_call x1, Pallas kernels, body(): pl.pallas_call(kernel, out_shape=(jax.ShapeDtypeStruct((STEPS, ROWS, COLS...  139 us

profile of v5, /device:TPU:1, one launch (start us, length us, event | category | flops | bytes accessed | tf_op | source)
XLA Modules:
  0.0 143.6 jit_solution(6221490821653033367)
XLA Ops:
  0.6 0.0 copy-start.2
  0.6 0.0 copy-start
  0.7 139.3 %steps.1 = (f32[4,56,256]{2,1,0:T(8,128)}, f32[512,256]{1,0:T(8,128)}) custom-call(s32[4]{0:T(128)} %order_ref.1, f32[32]{0:T(128)} %rate_hbm.1, f32[32]{0:T(128)} %penalty_hbm.1, bf16[512,896]{1,0:T(8,128)(2,1)} %acts_ref.1, f32[512,256]{1,0:T(8,128)} %resid_ref.1, bf16[32,56,256]{2,1,0:T(8,128)(2,1)} %weights_ref.1), custom_call_target="tpu_custom_call" | custom-call | tf_op jit(solution)/shard_map/steps/pallas_call | solution.py:469
  140.0 0.0 copy-done.2
  140.0 0.0 copy-done
  140.0 0.0 copy-start.1
  140.0 0.9 copy-done.1
  140.9 0.0 copy-start.3
  140.9 1.9 %place.1 = f32[32,56,256]{2,1,0:T(8,128)} custom-call(s32[4]{0:T(128)S(1)} %copy-done.2, bf16[32,56,256]{2,1,0:T(8,128)(2,1)S(1)} %copy-done, f32[4,56,256]{2,1,0:T(8,128)S(1)} %copy-done.1), custom_call_target="tpu_custom_call" | custom-call | tf_op jit(solution)/shard_map/place/pallas_call | solution.py:513
  142.8 0.0 copy-done.3
  142.8 0.8 copy.9
Async XLA Ops:
  0.6 139.3 %copy-start.2 = (s32[4]{0:T(128)S(1)}, s32[4]{0:T(128)}, u32[]{:S(2)}) copy-start(s32[4]{0:T(128)} %order_ref.1) | copy-start | bytes 52
  0.6 139.3 %copy-start = (bf16[32,56,256]{2,1,0:T(8,128)(2,1)S(1)}, bf16[32,56,256]{2,1,0:T(8,128)(2,1)}, u32[]{:S(2)}) copy-start(bf16[32,56,256]{2,1,0:T(8,128)(2,1)} %weights_ref.1) | copy-start | bytes 2752516
  140.0 0.9 copy-start.1
  140.9 1.9 %copy-start.3 = (f32[512,256]{1,0:T(8,128)S(1)}, f32[512,256]{1,0:T(8,128)}, u32[]{:S(2)}) copy-start(f32[512,256]{1,0:T(8,128)} %get-tuple-element.9) | copy-start | bytes 1572868
